TPU v7x, 32 devices: a whole 2x2x4 slice. The times are simulated.
32 devices in a mesh: span: 2 (over x), pitch: 4 (over y, core), chord: 4 (over z).
Axes of the slice: x: 2, y: 2, z: 4, core: 2. Of those that a mesh axis runs over, the one named last changes fastest.
Arguments:
- adjoint_start: float32 [3, 32, 128, 512], P(None, 'span', 'pitch', 'chord'), may hold values from -6 to 6
- sensitivity_source: float32 [3, 32, 128, 512], P(None, 'span', 'pitch', 'chord'), may hold values from -6 to 6
- stiffness_class: int32 [32, 128, 512], P('span', 'pitch', 'chord'), may hold values from 0 to 7
- stiffness_table: float32 [8], replicated, may hold values from 0.25 to 4
- wall_cell: int32 [32768], P(('span', 'pitch', 'chord')), may hold values from 0 to 65535
- patch_owner: int32 [32768, 1], P(('span', 'pitch', 'chord')), may hold values from 0 to 511; in each aligned block of 1024 rows (0 to 1023, 1024 to 2047, ...) at most 4 rows name the same one
- wall_normal: float32 [3, 32768], P(None, ('span', 'pitch', 'chord')), may hold values from -1 to 1
- mode_shape: float32 [8, 32768], P(None, ('span', 'pitch', 'chord')), may hold values from -6 to 6
Outputs:
- adjoint: float32 [3, 32, 128, 512], P(None, 'span', 'pitch', 'chord')
- patch_grad: float32 [8, 4096], P(None, ('span', 'pitch', 'chord'))
Inputs may be any that keep to these rules, and one draw needn't show every extreme that they name: `patch_owner`: within the rows of one device, no patch is named by more than 4 rows, a bound that some block reaches.
All inputs are finite; a program needn't handle non-finite values.
Results may differ from a plain program's by a relative error of at most 0.00018.
Values sent between devices are 32-bit elements; how exact they have to be, the bound alone decides.
A program may use at most 64 MiB of HBM per device.

v0:
```python
import math

import jax
import jax.numpy as jnp
from jax import lax
from jax.sharding import PartitionSpec as P

PATCH_DEV = 128
CAP = 4
MODES = 8
SWEEPS = 3


MASS_SHIFT = 0.5
RELAXATION = 0.8
DIAGONAL_SUM = 10.5
LAME_WEIGHTS = ((3.0, 1.0, 1.0), (1.0, 3.0, 1.0), (1.0, 1.0, 3.0))


def with_halo(x, sides, width):
    for axis, dim in sides:
        size, length = (lax.axis_size(axis), x.shape[dim])
        up = [(i, (i + 1) % size) for i in range(size - 1)]
        down = [(j, i) for i, j in up]
        last = lax.slice_in_dim(x, length - width, length, axis=dim)
        leading = lax.slice_in_dim(x, 0, width, axis=dim)
        before = lax.ppermute(last, axis, up)
        after = lax.ppermute(leading, axis, down)
        x = jnp.concatenate([before, x, after], axis=dim)
    return x


def stiffness_from(classes, table):
    result = jnp.zeros(classes.shape, jnp.float32)
    for number in range(table.shape[0]):
        result = result + jnp.where(classes == number, table[number], 0.0)
    return result


def operator_image(padded):
    center = padded[:, 1:-1, 1:-1, 1:-1]
    along_span = 2.0 * center - padded[:, 2:, 1:-1, 1:-1] - padded[:, :-2, 1:-1, 1:-1]
    along_pitch = 2.0 * center - padded[:, 1:-1, 2:, 1:-1] - padded[:, 1:-1, :-2, 1:-1]
    along_chord = 2.0 * center - padded[:, 1:-1, 1:-1, 2:] - padded[:, 1:-1, 1:-1, :-2]
    weights = jnp.array(LAME_WEIGHTS, jnp.float32)
    image = MASS_SHIFT * center
    image = image + weights[:, 0][:, None, None, None] * along_span
    image = image + weights[:, 1][:, None, None, None] * along_pitch
    image = image + weights[:, 2][:, None, None, None] * along_chord
    return image


def relax_step(adjoint, source, stiffness, image):
    return adjoint + RELAXATION * (source - image) / (DIAGONAL_SUM * stiffness)


def pick_traction(field, wall_cell):
    depth = field.shape[3]
    planes = field.shape[1] * field.shape[2]
    plane_major = field.reshape(3, planes, depth).transpose(1, 0, 2).reshape(planes, 3 * depth)
    plane_index = wall_cell // depth
    depth_index = wall_cell % depth
    plane_onehot = (plane_index[:, None] == jnp.arange(planes, dtype=jnp.int32)[None]).astype(
        jnp.float32
    )
    selected = jnp.dot(
        plane_onehot,
        plane_major,
        precision=lax.Precision.HIGHEST,
        preferred_element_type=jnp.float32,
    )
    selected = selected.reshape(-1, 3, depth)
    depth_onehot = (depth_index[:, None] == jnp.arange(depth, dtype=jnp.int32)[None]).astype(
        jnp.float32
    )
    return jnp.sum(selected * depth_onehot[:, None, :], axis=2).T


def owner_weighted(contribution, owner_index, chord_count):
    owner_onehot = (
        owner_index[None, :] == jnp.arange(chord_count, dtype=jnp.int32)[:, None]
    ).astype(jnp.float32)
    weighted = contribution[:, None, :] * owner_onehot[None]
    return weighted.reshape(-1, contribution.shape[1])


def slot_ranks(target):
    total_rows = target.shape[0]
    block_rows = math.gcd(total_rows, 512)
    positions = jnp.arange(total_rows, dtype=jnp.int32)

    def earlier_equal(pieces):
        block_target, block_position = pieces
        matching = (block_target[:, None] == target[None]) & (
            positions[None] < block_position[:, None]
        )
        return jnp.sum(matching.astype(jnp.int32), axis=1)

    ranked = lax.map(
        earlier_equal, (target.reshape(-1, block_rows), positions.reshape(-1, block_rows))
    )
    return ranked.reshape(total_rows)


def body(
    adjoint_start,
    sensitivity_source,
    stiffness_class,
    stiffness_table,
    wall_cell,
    patch_owner,
    wall_normal,
    mode_shape,
):
    stiffness = stiffness_from(stiffness_class, stiffness_table)
    adjoint = adjoint_start
    for sweep_index in range(SWEEPS):
        product = stiffness[None] * adjoint
        padded = with_halo(product, (("span", 1), ("pitch", 2), ("chord", 3)), 1)
        adjoint = relax_step(adjoint, sensitivity_source, stiffness, operator_image(padded))
    traction = pick_traction(stiffness[None] * adjoint, wall_cell)
    normal_part = jnp.sum(wall_normal * traction, axis=0)
    contribution = mode_shape * normal_part[None]
    target = patch_owner[:, 0]
    chord_count = lax.axis_size("chord")
    owner_index = target // PATCH_DEV
    local_patch = target % PATCH_DEV
    weighted = owner_weighted(contribution, owner_index, chord_count)
    slot_index = local_patch * CAP + slot_ranks(target)
    slot_onehot = (
        slot_index[:, None] == jnp.arange(PATCH_DEV * CAP, dtype=jnp.int32)[None]
    ).astype(jnp.float32)
    buffer = jnp.dot(
        weighted, slot_onehot, precision=lax.Precision.HIGHEST, preferred_element_type=jnp.float32
    )
    buffer = buffer.reshape(MODES, chord_count, PATCH_DEV * CAP)
    arrived = lax.all_to_all(buffer, "chord", split_axis=1, concat_axis=1, tiled=True)
    patch_grad = arrived.reshape(MODES, chord_count, PATCH_DEV, CAP).sum(axis=(1, 3))
    return (adjoint, patch_grad)


def solution(mesh):
    in_specs = (
        P(None, "span", "pitch", "chord"),
        P(None, "span", "pitch", "chord"),
        P("span", "pitch", "chord"),
        P(),
        P(("span", "pitch", "chord")),
        P(("span", "pitch", "chord"), None),
        P(None, ("span", "pitch", "chord")),
        P(None, ("span", "pitch", "chord")),
    )
    out_specs = (P(None, "span", "pitch", "chord"), P(None, ("span", "pitch", "chord")))
    return jax.shard_map(body, mesh=mesh, in_specs=in_specs, out_specs=out_specs, check_vma=False)
```

profile of v0, /device:TPU:6, one launch (start us, length us, event | category | flops | bytes accessed | tf_op | source)
XLA Modules:
  0.0 125.4 jit_solution(5719076352598324399)
XLA Ops:
  0.6 1.6 %fusion.81 = (f32[1]{0:T(128)}, f32[1]{0:T(128)}, f32[1]{0:T(128)}, f32[1]{0:T(128)}, f32[1]{0:T(128)}, /*index=5*/f32[1]{0:T(128)}, f32[1]{0:T(128)}, f32[1]{0:T(128)}) fusion(f32[8]{0:T(128)} %param.16), kind=kLoop, calls=%fused_computation.174 | loop fusion | bytes 64 | tf_op jit(solution)/shard_map/slice | solution.py:36
  2.3 6.2 %broadcast_multiply_fusion.4 = (f32[16,32,128]{2,1,0:T(8,128)S(1)}, f32[16,32,128]{2,1,0:T(8,128)S(1)}) fusion(f32[]{:T(128)} %bitcast.7, s32[16,32,128]{2,1,0:T(8,128)} %param.15, f32[]{:T(128)} %bitcast.6, f32[]{:T(128)} %bitcast.5, f32[]{:T(128)} %bitcast.4, f32[]{:T(128)} %bitcast.3, f32[]{:T(128)} %bitcast.2, f32[]{:T(128)} %bitcast.1, f32[]{:T(128)} %bitcast), kind=kLoop, calls=%fused_computation.129 | loop fusion | flops 1572864 | bytes 786464 | tf_op jit(solution)/shard_map/mul | solution.py:54
  8.5 0.1 broadcast_multiply_fusion.3
  8.6 2.4 %collective-permute-start = (f32[3,1,32,128]{3,2,1,0:T(8,128)S(1)}, f32[3,1,32,128]{3,2,1,0:T(8,128)S(1)}, u32[]{:S(2)}, u32[]{:S(2)}) collective-permute-start(f32[3,1,32,128]{3,2,1,0:T(8,128)S(1)} %get-tuple-element.88), channel_id=1, source_target_pairs={{16,0},{17,1},{18,2},{19,3},{20,4},{21,5},{22,6},{23,7},{24,8},{25... | collective-permute-start | bytes 147464 | tf_op jit(solution)/shard_map/ppermute | solution.py:28
  11.0 1.3 %collective-permute-start.1 = (f32[3,1,32,128]{3,2,1,0:T(8,128)S(1)}, f32[3,1,32,128]{3,2,1,0:T(8,128)S(1)}, u32[]{:S(2)}, u32[]{:S(2)}) collective-permute-start(f32[3,1,32,128]{3,2,1,0:T(8,128)S(1)} %get-tuple-element.87), channel_id=1, source_target_pairs={{0,16},{1,17},{2,18},{3,19},{4,20},{5,21},{6,22},{7,23},{8,24},{9,... | collective-permute-start | bytes 147464 | tf_op jit(solution)/shard_map/ppermute | solution.py:27
  12.3 0.4 collective-permute-done
  12.8 4.3 %collective-permute-done.1 = f32[3,1,32,128]{3,2,1,0:T(8,128)S(1)} collective-permute-done((f32[3,1,32,128]{3,2,1,0:T(8,128)S(1)}, f32[3,1,32,128]{3,2,1,0:T(8,128)S(1)}, u32[]{:S(2)}, u32[]{:S(2)}) %collective-permute-start.1) | collective-permute-done | bytes 49184 | tf_op jit(solution)/shard_map/ppermute | solution.py:27
  17.1 1.9 %collective-permute-start.2 = (f32[3,18,1,128]{3,2,1,0:T(1,128)S(1)}, f32[3,18,1,128]{3,2,1,0:T(1,128)S(1)}, u32[]{:S(2)}, u32[]{:S(2)}) collective-permute-start(f32[3,18,1,128]{3,2,1,0:T(1,128)S(1)} %get-tuple-element.82), channel_id=1, source_target_pairs={{4,0},{8,4},{12,8},{5,1},{9,5},{13,9},{6,2},{10,6},{14,10},{7,3},{... | collective-permute-start | bytes 82952 | tf_op jit(solution)/shard_map/ppermute | solution.py:28
  19.0 2.4 %collective-permute-start.3 = (f32[3,18,1,128]{3,2,1,0:T(1,128)S(1)}, f32[3,18,1,128]{3,2,1,0:T(1,128)S(1)}, u32[]{:S(2)}, u32[]{:S(2)}) collective-permute-start(f32[3,18,1,128]{3,2,1,0:T(1,128)S(1)} %get-tuple-element.81), channel_id=1, source_target_pairs={{0,4},{4,8},{8,12},{1,5},{5,9},{9,13},{2,6},{6,10},{10,14},{3,7},{... | collective-permute-start | bytes 82952 | tf_op jit(solution)/shard_map/ppermute | solution.py:27
  21.4 2.8 %collective-permute-done.3 = f32[3,18,1,128]{3,2,1,0:T(1,128)S(1)} collective-permute-done((f32[3,18,1,128]{3,2,1,0:T(1,128)S(1)}, f32[3,18,1,128]{3,2,1,0:T(1,128)S(1)}, u32[]{:S(2)}, u32[]{:S(2)}) %collective-permute-start.3) | collective-permute-done | bytes 27680 | tf_op jit(solution)/shard_map/ppermute | solution.py:27
  24.2 0.2 pad_maximum_fusion
  24.3 1.7 %fusion.77 = (f32[3,18,34,1]{3,2,1,0:T(8,128)}, f32[3,18,34,1]{3,2,1,0:T(8,128)}) fusion(f32[3,18,34,128]{3,2,1,0:T(8,128)S(1)} %pad_maximum_fusion), kind=kLoop, calls=%fused_computation.170 | loop fusion | bytes 29376 | tf_op jit(solution)/shard_map/slice | solution.py:26
  26.1 1.8 %copy.30 = f32[3,18,34,1]{2,3,1,0:T(1,128)S(1)} copy(f32[3,18,34,1]{3,2,1,0:T(8,128)} %get-tuple-element.75) | data formatting | bytes 14688 | tf_op jit(solution)/shard_map/slice | solution.py:26
  27.9 1.3 %collective-permute-start.4 = (f32[3,18,34,1]{2,3,1,0:T(1,128)S(1)}, f32[3,18,34,1]{2,3,1,0:T(1,128)S(1)}, u32[]{:S(2)}, u32[]{:S(2)}) collective-permute-start(f32[3,18,34,1]{2,3,1,0:T(1,128)S(1)} %copy.30), channel_id=1, source_target_pairs={{1,0},{2,1},{3,2},{5,4},{6,5},{7,6},{9,8},{10,9},{11,10},{13,12},{... | collective-permute-start | bytes 22040 | tf_op jit(solution)/shard_map/ppermute | solution.py:28
  29.2 0.5 copy.32
  29.6 4.5 %collective-permute-start.5 = (f32[3,18,34,1]{2,3,1,0:T(1,128)S(1)}, f32[3,18,34,1]{2,3,1,0:T(1,128)S(1)}, u32[]{:S(2)}, u32[]{:S(2)}) collective-permute-start(f32[3,18,34,1]{2,3,1,0:T(1,128)S(1)} %copy.32), channel_id=1, source_target_pairs={{0,1},{1,2},{2,3},{4,5},{5,6},{6,7},{8,9},{9,10},{10,11},{12,13},{... | collective-permute-start | bytes 22040 | tf_op jit(solution)/shard_map/ppermute | solution.py:27
  34.2 0.5 broadcast.122
  34.7 0.7 reduce.5
  35.4 0.0 copy-start.8
  35.5 1.5 %copy.31 = f32[3,18,34,1]{3,2,1,0:T(8,128)} copy(f32[3,18,34,1]{2,3,1,0:T(1,128)S(1)} %collective-permute-done.4) | data formatting | bytes 14688 | tf_op jit(solution)/shard_map/ppermute | solution.py:28
  37.0 1.5 %copy.33 = f32[3,18,34,1]{3,2,1,0:T(8,128)} copy(f32[3,18,34,1]{2,3,1,0:T(1,128)S(1)} %collective-permute-done.5) | data formatting | bytes 14688 | tf_op jit(solution)/shard_map/ppermute | solution.py:27
  38.5 4.5 %broadcast_multiply_fusion.2 = (f32[3,16,32,128]{3,2,1,0:T(8,128)S(1)}, f32[3,16,32,128]{3,2,1,0:T(8,128)}) fusion(f32[16,32,128]{2,1,0:T(8,128)S(1)} %get-tuple-element.68, f32[3,16,32,128]{3,2,1,0:T(8,128)} %param.13, f32[16,32,128]{2,1,0:T(8,128)S(1)} %get-tuple-element.67, f32[3,16,32,128]{3,2,1,0:T(8,128)S(1)} %copy-done, ...), kind=kLoop, calls=%fused_computation.125 | loop fusion | flops 7274496 | bytes 4624772 | tf_op jit(solution)/shard_map/mul | solution.py:118
  43.0 1.6 %collective-permute-start.6 = (f32[3,1,32,128]{3,2,1,0:T(8,128)S(1)}, f32[3,1,32,128]{3,2,1,0:T(8,128)S(1)}, u32[]{:S(2)}, u32[]{:S(2)}) collective-permute-start(f32[3,1,32,128]{3,2,1,0:T(8,128)S(1)} %get-tuple-element.86), channel_id=1, source_target_pairs={{16,0},{17,1},{18,2},{19,3},{20,4},{21,5},{22,6},{23,7},{24,8},{25... | collective-permute-start | bytes 147464 | tf_op jit(solution)/shard_map/ppermute | solution.py:28
  44.6 1.3 %collective-permute-start.7 = (f32[3,1,32,128]{3,2,1,0:T(8,128)S(1)}, f32[3,1,32,128]{3,2,1,0:T(8,128)S(1)}, u32[]{:S(2)}, u32[]{:S(2)}) collective-permute-start(f32[3,1,32,128]{3,2,1,0:T(8,128)S(1)} %get-tuple-element.85), channel_id=1, source_target_pairs={{0,16},{1,17},{2,18},{3,19},{4,20},{5,21},{6,22},{7,23},{8,24},{9,... | collective-permute-start | bytes 147464 | tf_op jit(solution)/shard_map/ppermute | solution.py:27
  45.9 1.4 %while.11 = (s32[]{:T(128)}, s32[2,512]{1,0:T(2,128)S(1)}, s32[2,512]{1,0:T(2,128)S(1)}, s32[1024,1]{0,1:T(1,128)S(1)}, s32[2,512]{1,0:T(2,128)S(1)}, /*index=5*/s32[]{:T(128)}, s32[]{:T(128)}) while((s32[]{:T(128)}, s32[2,512]{1,0:T(2,128)S(1)}, s32[2,512]{1,0:T(2,128)S(1)}, s32[1024,1]{0,1:T(1,128)S(1)}, s32[2,512]{1,0:T(2,128)S(1)}, ...), condition=%wide.region_4.5_spmd.clone, body=%wide.region_2.4_spmd.clone.sunk | while | flops 2620930 | bytes 22613 | solution.py:99
  46.0 0.6 convert_reduce_fusion.2
  46.7 0.6 convert_reduce_fusion.2
  47.4 3.3 %collective-permute-done.7 = f32[3,1,32,128]{3,2,1,0:T(8,128)S(1)} collective-permute-done((f32[3,1,32,128]{3,2,1,0:T(8,128)S(1)}, f32[3,1,32,128]{3,2,1,0:T(8,128)S(1)}, u32[]{:S(2)}, u32[]{:S(2)}) %collective-permute-start.7) | collective-permute-done | bytes 49184 | tf_op jit(solution)/shard_map/ppermute | solution.py:27
  50.7 1.9 %collective-permute-start.8 = (f32[3,18,1,128]{3,2,1,0:T(1,128)S(1)}, f32[3,18,1,128]{3,2,1,0:T(1,128)S(1)}, u32[]{:S(2)}, u32[]{:S(2)}) collective-permute-start(f32[3,18,1,128]{3,2,1,0:T(1,128)S(1)} %get-tuple-element.80), channel_id=1, source_target_pairs={{4,0},{8,4},{12,8},{5,1},{9,5},{13,9},{6,2},{10,6},{14,10},{7,3},{... | collective-permute-start | bytes 82952 | tf_op jit(solution)/shard_map/ppermute | solution.py:28
  52.6 2.4 %collective-permute-start.9 = (f32[3,18,1,128]{3,2,1,0:T(1,128)S(1)}, f32[3,18,1,128]{3,2,1,0:T(1,128)S(1)}, u32[]{:S(2)}, u32[]{:S(2)}) collective-permute-start(f32[3,18,1,128]{3,2,1,0:T(1,128)S(1)} %get-tuple-element.79), channel_id=1, source_target_pairs={{0,4},{4,8},{8,12},{1,5},{5,9},{9,13},{2,6},{6,10},{10,14},{3,7},{... | collective-permute-start | bytes 82952 | tf_op jit(solution)/shard_map/ppermute | solution.py:27
  55.1 2.7 %collective-permute-done.9 = f32[3,18,1,128]{3,2,1,0:T(1,128)S(1)} collective-permute-done((f32[3,18,1,128]{3,2,1,0:T(1,128)S(1)}, f32[3,18,1,128]{3,2,1,0:T(1,128)S(1)}, u32[]{:S(2)}, u32[]{:S(2)}) %collective-permute-start.9) | collective-permute-done | bytes 27680 | tf_op jit(solution)/shard_map/ppermute | solution.py:27
  57.8 0.2 pad_maximum_fusion.1
  57.9 1.4 %fusion.76 = (f32[3,18,34,1]{3,2,1,0:T(8,128)}, f32[3,18,34,1]{3,2,1,0:T(8,128)S(1)}) fusion(f32[3,18,34,128]{3,2,1,0:T(8,128)S(1)} %pad_maximum_fusion.1), kind=kLoop, calls=%fused_computation.169 | loop fusion | bytes 29376 | tf_op jit(solution)/shard_map/slice | solution.py:26
  59.3 1.7 %copy.34 = f32[3,18,34,1]{2,3,1,0:T(1,128)S(1)} copy(f32[3,18,34,1]{3,2,1,0:T(8,128)} %get-tuple-element.73) | data formatting | bytes 14688 | tf_op jit(solution)/shard_map/slice | solution.py:26
  61.0 1.3 %collective-permute-start.10 = (f32[3,18,34,1]{2,3,1,0:T(1,128)S(1)}, f32[3,18,34,1]{2,3,1,0:T(1,128)S(1)}, u32[]{:S(2)}, u32[]{:S(2)}) collective-permute-start(f32[3,18,34,1]{2,3,1,0:T(1,128)S(1)} %copy.34), channel_id=1, source_target_pairs={{1,0},{2,1},{3,2},{5,4},{6,5},{7,6},{9,8},{10,9},{11,10},{13,12},{... | collective-permute-start | bytes 22040 | tf_op jit(solution)/shard_map/ppermute | solution.py:28
  62.3 0.5 copy.36
  62.8 4.5 %collective-permute-start.11 = (f32[3,18,34,1]{2,3,1,0:T(1,128)S(1)}, f32[3,18,34,1]{2,3,1,0:T(1,128)S(1)}, u32[]{:S(2)}, u32[]{:S(2)}) collective-permute-start(f32[3,18,34,1]{2,3,1,0:T(1,128)S(1)} %copy.36), channel_id=1, source_target_pairs={{0,1},{1,2},{2,3},{4,5},{5,6},{6,7},{8,9},{9,10},{10,11},{12,13},{... | collective-permute-start | bytes 22040 | tf_op jit(solution)/shard_map/ppermute | solution.py:27
  67.3 0.8 fusion.59
  68.2 1.5 %copy.35 = f32[3,18,34,1]{3,2,1,0:T(8,128)} copy(f32[3,18,34,1]{2,3,1,0:T(1,128)S(1)} %collective-permute-done.10) | data formatting | bytes 14688 | tf_op jit(solution)/shard_map/ppermute | solution.py:28
  69.7 1.5 %copy.37 = f32[3,18,34,1]{3,2,1,0:T(8,128)} copy(f32[3,18,34,1]{2,3,1,0:T(1,128)S(1)} %collective-permute-done.11) | data formatting | bytes 14688 | tf_op jit(solution)/shard_map/ppermute | solution.py:27
  71.2 4.5 %broadcast_multiply_fusion.1 = (f32[3,16,32,128]{3,2,1,0:T(8,128)S(1)}, f32[3,16,32,128]{3,2,1,0:T(8,128)}) fusion(f32[16,32,128]{2,1,0:T(8,128)S(1)} %get-tuple-element.68, f32[3,16,32,128]{3,2,1,0:T(8,128)} %get-tuple-element.66, f32[16,32,128]{2,1,0:T(8,128)S(1)} %get-tuple-element.67, f32[3,16,32,128]{3,2,1,0:T(8,128)S(1)} %copy-done, ...), kind=kLoop, calls=%fused_computation.124 | loop fusion | flops 7274496 | bytes 4624772 | tf_op jit(solution)/shard_map/mul | solution.py:118
  75.7 1.6 %collective-permute-start.12 = (f32[3,1,32,128]{3,2,1,0:T(8,128)S(1)}, f32[3,1,32,128]{3,2,1,0:T(8,128)S(1)}, u32[]{:S(2)}, u32[]{:S(2)}) collective-permute-start(f32[3,1,32,128]{3,2,1,0:T(8,128)S(1)} %get-tuple-element.84), channel_id=1, source_target_pairs={{16,0},{17,1},{18,2},{19,3},{20,4},{21,5},{22,6},{23,7},{24,8},{25... | collective-permute-start | bytes 147464 | tf_op jit(solution)/shard_map/ppermute | solution.py:28
  77.3 1.3 %collective-permute-start.13 = (f32[3,1,32,128]{3,2,1,0:T(8,128)S(1)}, f32[3,1,32,128]{3,2,1,0:T(8,128)S(1)}, u32[]{:S(2)}, u32[]{:S(2)}) collective-permute-start(f32[3,1,32,128]{3,2,1,0:T(8,128)S(1)} %get-tuple-element.83), channel_id=1, source_target_pairs={{0,16},{1,17},{2,18},{3,19},{4,20},{5,21},{6,22},{7,23},{8,24},{9,... | collective-permute-start | bytes 147464 | tf_op jit(solution)/shard_map/ppermute | solution.py:27
  78.6 0.4 collective-permute-done.12
  79.0 4.3 %collective-permute-done.13 = f32[3,1,32,128]{3,2,1,0:T(8,128)S(1)} collective-permute-done((f32[3,1,32,128]{3,2,1,0:T(8,128)S(1)}, f32[3,1,32,128]{3,2,1,0:T(8,128)S(1)}, u32[]{:S(2)}, u32[]{:S(2)}) %collective-permute-start.13) | collective-permute-done | bytes 49184 | tf_op jit(solution)/shard_map/ppermute | solution.py:27
  83.3 1.9 %collective-permute-start.14 = (f32[3,18,1,128]{3,2,1,0:T(1,128)S(1)}, f32[3,18,1,128]{3,2,1,0:T(1,128)S(1)}, u32[]{:S(2)}, u32[]{:S(2)}) collective-permute-start(f32[3,18,1,128]{3,2,1,0:T(1,128)S(1)} %get-tuple-element.78), channel_id=1, source_target_pairs={{4,0},{8,4},{12,8},{5,1},{9,5},{13,9},{6,2},{10,6},{14,10},{7,3},{... | collective-permute-start | bytes 82952 | tf_op jit(solution)/shard_map/ppermute | solution.py:28
  85.2 2.4 %collective-permute-start.15 = (f32[3,18,1,128]{3,2,1,0:T(1,128)S(1)}, f32[3,18,1,128]{3,2,1,0:T(1,128)S(1)}, u32[]{:S(2)}, u32[]{:S(2)}) collective-permute-start(f32[3,18,1,128]{3,2,1,0:T(1,128)S(1)} %get-tuple-element.77), channel_id=1, source_target_pairs={{0,4},{4,8},{8,12},{1,5},{5,9},{9,13},{2,6},{6,10},{10,14},{3,7},{... | collective-permute-start | bytes 82952 | tf_op jit(solution)/shard_map/ppermute | solution.py:27
  87.7 2.7 %collective-permute-done.15 = f32[3,18,1,128]{3,2,1,0:T(1,128)S(1)} collective-permute-done((f32[3,18,1,128]{3,2,1,0:T(1,128)S(1)}, f32[3,18,1,128]{3,2,1,0:T(1,128)S(1)}, u32[]{:S(2)}, u32[]{:S(2)}) %collective-permute-start.15) | collective-permute-done | bytes 27680 | tf_op jit(solution)/shard_map/ppermute | solution.py:27
  90.4 0.2 pad_maximum_fusion.2
  90.6 1.7 %fusion.75 = (f32[3,18,34,1]{3,2,1,0:T(8,128)}, f32[3,18,34,1]{3,2,1,0:T(8,128)}) fusion(f32[3,18,34,128]{3,2,1,0:T(8,128)S(1)} %pad_maximum_fusion.2), kind=kLoop, calls=%fused_computation.168 | loop fusion | bytes 29376 | tf_op jit(solution)/shard_map/slice | solution.py:26
  92.3 1.7 %copy.38 = f32[3,18,34,1]{2,3,1,0:T(1,128)S(1)} copy(f32[3,18,34,1]{3,2,1,0:T(8,128)} %get-tuple-element.71) | data formatting | bytes 14688 | tf_op jit(solution)/shard_map/slice | solution.py:26
  94.0 1.3 %collective-permute-start.16 = (f32[3,18,34,1]{2,3,1,0:T(1,128)S(1)}, f32[3,18,34,1]{2,3,1,0:T(1,128)S(1)}, u32[]{:S(2)}, u32[]{:S(2)}) collective-permute-start(f32[3,18,34,1]{2,3,1,0:T(1,128)S(1)} %copy.38), channel_id=1, source_target_pairs={{1,0},{2,1},{3,2},{5,4},{6,5},{7,6},{9,8},{10,9},{11,10},{13,12},{... | collective-permute-start | bytes 22040 | tf_op jit(solution)/shard_map/ppermute | solution.py:28
  95.3 1.7 %copy.40 = f32[3,18,34,1]{2,3,1,0:T(1,128)S(1)} copy(f32[3,18,34,1]{3,2,1,0:T(8,128)} %get-tuple-element.72) | data formatting | bytes 14688 | tf_op jit(solution)/shard_map/slice | solution.py:25
  97.0 4.7 %collective-permute-start.17 = (f32[3,18,34,1]{2,3,1,0:T(1,128)S(1)}, f32[3,18,34,1]{2,3,1,0:T(1,128)S(1)}, u32[]{:S(2)}, u32[]{:S(2)}) collective-permute-start(f32[3,18,34,1]{2,3,1,0:T(1,128)S(1)} %copy.40), channel_id=1, source_target_pairs={{0,1},{1,2},{2,3},{4,5},{5,6},{6,7},{8,9},{9,10},{10,11},{12,13},{... | collective-permute-start | bytes 22040 | tf_op jit(solution)/shard_map/ppermute | solution.py:27
  101.8 1.5 %copy.39 = f32[3,18,34,1]{3,2,1,0:T(8,128)} copy(f32[3,18,34,1]{2,3,1,0:T(1,128)S(1)} %collective-permute-done.16) | data formatting | bytes 14688 | tf_op jit(solution)/shard_map/ppermute | solution.py:28
  103.3 1.5 %copy.41 = f32[3,18,34,1]{3,2,1,0:T(8,128)} copy(f32[3,18,34,1]{2,3,1,0:T(1,128)S(1)} %collective-permute-done.17) | data formatting | bytes 14688 | tf_op jit(solution)/shard_map/ppermute | solution.py:27
  104.8 4.5 %broadcast_multiply_fusion = (f32[3,16,32,128]{3,2,1,0:T(8,128)}, f32[3,16,32,128]{3,2,1,0:T(8,128)}) fusion(f32[16,32,128]{2,1,0:T(8,128)S(1)} %get-tuple-element.68, f32[3,16,32,128]{3,2,1,0:T(8,128)S(1)} %copy-done.3, f32[16,32,128]{2,1,0:T(8,128)S(1)} %get-tuple-element.67, f32[3,16,32,128]{3,2,1,0:T(8,128)S(1)} %copy-done, ...), kind=kLoop, calls=%fused_computation.123 | loop fusion | flops 7274496 | bytes 4624772 | tf_op jit(solution)/shard_map/mul | solution.py:121
  109.4 1.5 %copy.42 = f32[512,3,128]{0,2,1:T(8,128)S(1)} copy(f32[512,3,128]{2,0,1:T(8,128)} %bitcast.50) | data formatting | bytes 1572864 | tf_op jit(solution)/shard_map/transpose | solution.py:60
  110.9 1.7 %multiply_reduce_fusion = f32[1024,3]{0,1:T(4,128)S(1)} fusion(s32[1024]{0:T(1024)S(1)} %get-tuple-element.90, f32[512,3,128]{0,2,1:T(8,128)S(1)} %copy.42, f32[1024,128]{0,1:T(8,128)S(1)} %copy-done.4), kind=kOutput, calls=%fused_computation.12 | convolution fusion | flops 2417226752 | bytes 1327104 | tf_op jit(solution)/shard_map/dot_general | solution.py:66
  112.6 0.9 fusion.7
  113.5 11.0 %all_to_all.5 = f32[8,4,512]{2,0,1:T(8,128)S(1)} all-to-all(f32[8,4,512]{2,0,1:T(8,128)S(1)} %fusion.7), channel_id=1, replica_groups=mesh['span'=2,'pitch'=4,'chord'=4] {'chord'}, dimensions={1} | all-to-all | bytes 131072 | tf_op jit(solution)/shard_map/all_to_all | solution.py:137
  124.4 0.1 copy.43
  124.6 0.2 reduce_sum.47
  124.7 0.7 copy.44
  (54 shorter events, 0.4 us)
Async XLA Ops:
  0.6 7.8 %copy-start.2 = (f32[3,16,32,128]{3,2,1,0:T(8,128)S(1)}, f32[3,16,32,128]{3,2,1,0:T(8,128)}, u32[]{:S(2)}) copy-start(f32[3,16,32,128]{3,2,1,0:T(8,128)} %param.13) | copy-start | bytes 2359300
  8.6 4.2 %collective-permute-start = (f32[3,1,32,128]{3,2,1,0:T(8,128)S(1)}, f32[3,1,32,128]{3,2,1,0:T(8,128)S(1)}, u32[]{:S(2)}, u32[]{:S(2)}) collective-permute-start(f32[3,1,32,128]{3,2,1,0:T(8,128)S(1)} %get-tuple-element.88), channel_id=1, source_target_pairs={{16,0},{17,1},{18,2},{19,3},{20,4},{21,5},{22,6},{23,7},{24,8},{25... | collective-permute-start | bytes 147464 | tf_op jit(solution)/shard_map/ppermute | solution.py:28
  11.0 6.0 %collective-permute-start.1 = (f32[3,1,32,128]{3,2,1,0:T(8,128)S(1)}, f32[3,1,32,128]{3,2,1,0:T(8,128)S(1)}, u32[]{:S(2)}, u32[]{:S(2)}) collective-permute-start(f32[3,1,32,128]{3,2,1,0:T(8,128)S(1)} %get-tuple-element.87), channel_id=1, source_target_pairs={{0,16},{1,17},{2,18},{3,19},{4,20},{5,21},{6,22},{7,23},{8,24},{9,... | collective-permute-start | bytes 147464 | tf_op jit(solution)/shard_map/ppermute | solution.py:27
  17.1 4.3 %collective-permute-start.2 = (f32[3,18,1,128]{3,2,1,0:T(1,128)S(1)}, f32[3,18,1,128]{3,2,1,0:T(1,128)S(1)}, u32[]{:S(2)}, u32[]{:S(2)}) collective-permute-start(f32[3,18,1,128]{3,2,1,0:T(1,128)S(1)} %get-tuple-element.82), channel_id=1, source_target_pairs={{4,0},{8,4},{12,8},{5,1},{9,5},{13,9},{6,2},{10,6},{14,10},{7,3},{... | collective-permute-start | bytes 82952 | tf_op jit(solution)/shard_map/ppermute | solution.py:28
  19.0 5.2 %collective-permute-start.3 = (f32[3,18,1,128]{3,2,1,0:T(1,128)S(1)}, f32[3,18,1,128]{3,2,1,0:T(1,128)S(1)}, u32[]{:S(2)}, u32[]{:S(2)}) collective-permute-start(f32[3,18,1,128]{3,2,1,0:T(1,128)S(1)} %get-tuple-element.81), channel_id=1, source_target_pairs={{0,4},{4,8},{8,12},{1,5},{5,9},{9,13},{2,6},{6,10},{10,14},{3,7},{... | collective-permute-start | bytes 82952 | tf_op jit(solution)/shard_map/ppermute | solution.py:27
  26.1 3.1 %copy-start.1 = (f32[3,18,34,1]{3,2,1,0:T(8,128)S(1)}, f32[3,18,34,1]{3,2,1,0:T(8,128)}, u32[]{:S(2)}) copy-start(f32[3,18,34,1]{3,2,1,0:T(8,128)} %get-tuple-element.76) | copy-start | bytes 22036
  26.1 8.7 %copy-start.5 = (s32[1024,1]{0,1:T(1,128)S(1)}, s32[1024,1]{0,1:T(1,128)}, u32[]{:S(2)}) copy-start(s32[1024,1]{0,1:T(1,128)} %param.18) | copy-start | bytes 12292
  27.9 7.6 %collective-permute-start.4 = (f32[3,18,34,1]{2,3,1,0:T(1,128)S(1)}, f32[3,18,34,1]{2,3,1,0:T(1,128)S(1)}, u32[]{:S(2)}, u32[]{:S(2)}) collective-permute-start(f32[3,18,34,1]{2,3,1,0:T(1,128)S(1)} %copy.30), channel_id=1, source_target_pairs={{1,0},{2,1},{3,2},{5,4},{6,5},{7,6},{9,8},{10,9},{11,10},{13,12},{... | collective-permute-start | bytes 22040 | tf_op jit(solution)/shard_map/ppermute | solution.py:28
  29.6 7.3 %collective-permute-start.5 = (f32[3,18,34,1]{2,3,1,0:T(1,128)S(1)}, f32[3,18,34,1]{2,3,1,0:T(1,128)S(1)}, u32[]{:S(2)}, u32[]{:S(2)}) collective-permute-start(f32[3,18,34,1]{2,3,1,0:T(1,128)S(1)} %copy.32), channel_id=1, source_target_pairs={{0,1},{1,2},{2,3},{4,5},{5,6},{6,7},{8,9},{9,10},{10,11},{12,13},{... | collective-permute-start | bytes 22040 | tf_op jit(solution)/shard_map/ppermute | solution.py:27
  35.4 3.1 %copy-start = (f32[3,16,32,128]{3,2,1,0:T(8,128)S(1)}, f32[3,16,32,128]{3,2,1,0:T(8,128)}, u32[]{:S(2)}) copy-start(f32[3,16,32,128]{3,2,1,0:T(8,128)} %param.14) | copy-start | bytes 2359300
  35.4 3.1 %copy-start.8 = (f32[3]{0:T(128)S(1)}, f32[3]{0:T(128)}, u32[]{:S(2)}) copy-start(f32[3]{0:T(128)} %constant.83) | copy-start | bytes 40
  35.4 3.0 %copy-start.9 = (f32[3]{0:T(128)S(1)}, f32[3]{0:T(128)}, u32[]{:S(2)}) copy-start(f32[3]{0:T(128)} %constant.85) | copy-start | bytes 40
  35.5 3.0 %copy-start.10 = (f32[3]{0:T(128)S(1)}, f32[3]{0:T(128)}, u32[]{:S(2)}) copy-start(f32[3]{0:T(128)} %constant.87) | copy-start | bytes 40
  43.0 12.0 %copy-start.11 = (s32[1024]{0:T(1024)S(1)}, s32[1024]{0:T(1024)}, u32[]{:S(2)}) copy-start(s32[1024]{0:T(1024)} %param.17) | copy-start | bytes 12292
  43.0 4.3 %collective-permute-start.6 = (f32[3,1,32,128]{3,2,1,0:T(8,128)S(1)}, f32[3,1,32,128]{3,2,1,0:T(8,128)S(1)}, u32[]{:S(2)}, u32[]{:S(2)}) collective-permute-start(f32[3,1,32,128]{3,2,1,0:T(8,128)S(1)} %get-tuple-element.86), channel_id=1, source_target_pairs={{16,0},{17,1},{18,2},{19,3},{20,4},{21,5},{22,6},{23,7},{24,8},{25... | collective-permute-start | bytes 147464 | tf_op jit(solution)/shard_map/ppermute | solution.py:28
  44.6 6.0 %collective-permute-start.7 = (f32[3,1,32,128]{3,2,1,0:T(8,128)S(1)}, f32[3,1,32,128]{3,2,1,0:T(8,128)S(1)}, u32[]{:S(2)}, u32[]{:S(2)}) collective-permute-start(f32[3,1,32,128]{3,2,1,0:T(8,128)S(1)} %get-tuple-element.85), channel_id=1, source_target_pairs={{0,16},{1,17},{2,18},{3,19},{4,20},{5,21},{6,22},{7,23},{8,24},{9,... | collective-permute-start | bytes 147464 | tf_op jit(solution)/shard_map/ppermute | solution.py:27
  50.7 4.4 %collective-permute-start.8 = (f32[3,18,1,128]{3,2,1,0:T(1,128)S(1)}, f32[3,18,1,128]{3,2,1,0:T(1,128)S(1)}, u32[]{:S(2)}, u32[]{:S(2)}) collective-permute-start(f32[3,18,1,128]{3,2,1,0:T(1,128)S(1)} %get-tuple-element.80), channel_id=1, source_target_pairs={{4,0},{8,4},{12,8},{5,1},{9,5},{13,9},{6,2},{10,6},{14,10},{7,3},{... | collective-permute-start | bytes 82952 | tf_op jit(solution)/shard_map/ppermute | solution.py:28
  52.6 5.2 %collective-permute-start.9 = (f32[3,18,1,128]{3,2,1,0:T(1,128)S(1)}, f32[3,18,1,128]{3,2,1,0:T(1,128)S(1)}, u32[]{:S(2)}, u32[]{:S(2)}) collective-permute-start(f32[3,18,1,128]{3,2,1,0:T(1,128)S(1)} %get-tuple-element.79), channel_id=1, source_target_pairs={{0,4},{4,8},{8,12},{1,5},{5,9},{9,13},{2,6},{6,10},{10,14},{3,7},{... | collective-permute-start | bytes 82952 | tf_op jit(solution)/shard_map/ppermute | solution.py:27
  61.0 7.2 %collective-permute-start.10 = (f32[3,18,34,1]{2,3,1,0:T(1,128)S(1)}, f32[3,18,34,1]{2,3,1,0:T(1,128)S(1)}, u32[]{:S(2)}, u32[]{:S(2)}) collective-permute-start(f32[3,18,34,1]{2,3,1,0:T(1,128)S(1)} %copy.34), channel_id=1, source_target_pairs={{1,0},{2,1},{3,2},{5,4},{6,5},{7,6},{9,8},{10,9},{11,10},{13,12},{... | collective-permute-start | bytes 22040 | tf_op jit(solution)/shard_map/ppermute | solution.py:28
  62.8 6.9 %collective-permute-start.11 = (f32[3,18,34,1]{2,3,1,0:T(1,128)S(1)}, f32[3,18,34,1]{2,3,1,0:T(1,128)S(1)}, u32[]{:S(2)}, u32[]{:S(2)}) collective-permute-start(f32[3,18,34,1]{2,3,1,0:T(1,128)S(1)} %copy.36), channel_id=1, source_target_pairs={{0,1},{1,2},{2,3},{4,5},{5,6},{6,7},{8,9},{9,10},{10,11},{12,13},{... | collective-permute-start | bytes 22040 | tf_op jit(solution)/shard_map/ppermute | solution.py:27
  75.7 3.3 %collective-permute-start.12 = (f32[3,1,32,128]{3,2,1,0:T(8,128)S(1)}, f32[3,1,32,128]{3,2,1,0:T(8,128)S(1)}, u32[]{:S(2)}, u32[]{:S(2)}) collective-permute-start(f32[3,1,32,128]{3,2,1,0:T(8,128)S(1)} %get-tuple-element.84), channel_id=1, source_target_pairs={{16,0},{17,1},{18,2},{19,3},{20,4},{21,5},{22,6},{23,7},{24,8},{25... | collective-permute-start | bytes 147464 | tf_op jit(solution)/shard_map/ppermute | solution.py:28
  77.3 6.0 %collective-permute-start.13 = (f32[3,1,32,128]{3,2,1,0:T(8,128)S(1)}, f32[3,1,32,128]{3,2,1,0:T(8,128)S(1)}, u32[]{:S(2)}, u32[]{:S(2)}) collective-permute-start(f32[3,1,32,128]{3,2,1,0:T(8,128)S(1)} %get-tuple-element.83), channel_id=1, source_target_pairs={{0,16},{1,17},{2,18},{3,19},{4,20},{5,21},{6,22},{7,23},{8,24},{9,... | collective-permute-start | bytes 147464 | tf_op jit(solution)/shard_map/ppermute | solution.py:27
  83.3 4.4 %collective-permute-start.14 = (f32[3,18,1,128]{3,2,1,0:T(1,128)S(1)}, f32[3,18,1,128]{3,2,1,0:T(1,128)S(1)}, u32[]{:S(2)}, u32[]{:S(2)}) collective-permute-start(f32[3,18,1,128]{3,2,1,0:T(1,128)S(1)} %get-tuple-element.78), channel_id=1, source_target_pairs={{4,0},{8,4},{12,8},{5,1},{9,5},{13,9},{6,2},{10,6},{14,10},{7,3},{... | collective-permute-start | bytes 82952 | tf_op jit(solution)/shard_map/ppermute | solution.py:28
  85.2 5.2 %collective-permute-start.15 = (f32[3,18,1,128]{3,2,1,0:T(1,128)S(1)}, f32[3,18,1,128]{3,2,1,0:T(1,128)S(1)}, u32[]{:S(2)}, u32[]{:S(2)}) collective-permute-start(f32[3,18,1,128]{3,2,1,0:T(1,128)S(1)} %get-tuple-element.77), channel_id=1, source_target_pairs={{0,4},{4,8},{8,12},{1,5},{5,9},{9,13},{2,6},{6,10},{10,14},{3,7},{... | collective-permute-start | bytes 82952 | tf_op jit(solution)/shard_map/ppermute | solution.py:27
  94.0 7.8 %collective-permute-start.16 = (f32[3,18,34,1]{2,3,1,0:T(1,128)S(1)}, f32[3,18,34,1]{2,3,1,0:T(1,128)S(1)}, u32[]{:S(2)}, u32[]{:S(2)}) collective-permute-start(f32[3,18,34,1]{2,3,1,0:T(1,128)S(1)} %copy.38), channel_id=1, source_target_pairs={{1,0},{2,1},{3,2},{5,4},{6,5},{7,6},{9,8},{10,9},{11,10},{13,12},{... | collective-permute-start | bytes 22040 | tf_op jit(solution)/shard_map/ppermute | solution.py:28
  97.0 6.3 %collective-permute-start.17 = (f32[3,18,34,1]{2,3,1,0:T(1,128)S(1)}, f32[3,18,34,1]{2,3,1,0:T(1,128)S(1)}, u32[]{:S(2)}, u32[]{:S(2)}) collective-permute-start(f32[3,18,34,1]{2,3,1,0:T(1,128)S(1)} %copy.40), channel_id=1, source_target_pairs={{0,1},{1,2},{2,3},{4,5},{5,6},{6,7},{8,9},{9,10},{10,11},{12,13},{... | collective-permute-start | bytes 22040 | tf_op jit(solution)/shard_map/ppermute | solution.py:27
  101.8 3.0 %copy-start.3 = (f32[3,16,32,128]{3,2,1,0:T(8,128)S(1)}, f32[3,16,32,128]{3,2,1,0:T(8,128)}, u32[]{:S(2)}) copy-start(f32[3,16,32,128]{3,2,1,0:T(8,128)} %get-tuple-element.64) | copy-start | bytes 2359300
  109.4 1.5 %copy-start.4 = (f32[1024,128]{0,1:T(8,128)S(1)}, f32[1024,128]{0,1:T(8,128)}, u32[]{:S(2)}) copy-start(f32[1024,128]{0,1:T(8,128)} %fusion.59) | copy-start | bytes 1572868
  110.8 1.7 %copy-start.7 = (f32[3,1024]{1,0:T(4,128)S(1)}, f32[3,1024]{1,0:T(4,128)}, u32[]{:S(2)}) copy-start(f32[3,1024]{1,0:T(4,128)} %param.19) | copy-start | bytes 36868
  110.8 1.7 %copy-start.6 = (f32[8,1024]{1,0:T(8,128)S(1)}, f32[8,1024]{1,0:T(8,128)}, u32[]{:S(2)}) copy-start(f32[8,1024]{1,0:T(8,128)} %param.20) | copy-start | bytes 98308
where the time goes:
time: 126 us; the launch traced here: 125 us
  starting transfers between devices  40.1 us (32%)
  local copies, waits for them, and re-layouts  26.3 us (21%)
  other arithmetic  23.5 us (19%)
  waiting for transfers between devices  20.9 us (17%)
  blocking collectives  11 us (9%)
  matrix products  2.55 us (2%)
    ppermute x9, starting transfers between devices, with_halo(): before = lax.ppermute(last, axis, up)  24.9 us
    ppermute x9, waiting for transfers between devices, with_halo(): before = lax.ppermute(last, axis, up)  20 us
    ppermute x9, starting transfers between devices, with_halo(): after = lax.ppermute(leading, axis, down)  15.2 us
    all_to_all x1, blocking collectives, body(): lax.all_to_all(buffer, 'chord', split_axis=1, concat_axis=1, tiled=True)  11 us
    slice x6, local copies, waits for them, and re-layouts, with_halo(): leading = lax.slice_in_dim(x, 0, width, axis=dim)  10 us
    mul x3, other arithmetic, body(): product = stiffness[None] * adjoint  9.13 us
    mul x1, other arithmetic, relax_step(): return adjoint + RELAXATION * (source - image) / (DIAGONAL_SUM * stiffness)  6.19 us
    mul x1, other arithmetic, body(): traction = pick_traction(stiffness[None] * adjoint, wall_cell)  4.53 us
  transfers between devices with their start and end apart: 18, of which 8 were waited for; matrix products, arithmetic and copies ran while one was open for 8% of the time, Pallas kernels for 0%

commit v1 on v0

v1 whole, which is shorter than its diff:
```python
import functools

import jax
import jax.numpy as jnp
from jax import lax
from jax.experimental import pallas as pl
from jax.experimental.pallas import tpu as pltpu
from jax.sharding import PartitionSpec as P

MESH = pl.DeviceIdType.MESH
AXES = ("span", "pitch", "chord")
PATCH_DEV = 128
MODES = 8
SWEEPS = 3
RELAXATION = 0.8
DIAGONAL_SUM = 10.5
STEP = RELAXATION / DIAGONAL_SUM
KEEP = 1.0 - RELAXATION
OFF_WEIGHT = 1.0
OWN_WEIGHT = 3.0
F32 = jnp.float32
BF16 = jnp.bfloat16


def weight(component, dim):
    return OWN_WEIGHT if component == dim else OFF_WEIGHT


def split(value):
    high = value.astype(BF16)
    low = (value - high.astype(F32)).astype(BF16)
    return high, low


def kernel(
    sizes,
    start_hbm,
    source_hbm,
    class_hbm,
    table,
    cell_hbm,
    owner_hbm,
    normal_hbm,
    mode_hbm,
    adjoint_hbm,
    patch_out,
    start,
    source,
    classes,
    cell,
    owner,
    normal,
    mode,
    stiff,
    inverse,
    prod,
    halo_x,
    halo_y,
    halo_z,
    face_y,
    face_z,
    result,
    pieces,
    depth_hot,
    patch_hot,
    group_send,
    group_recv,
    in_sem,
    small_sem,
    out_sem,
    send_sem,
    recv_sem,
    group_send_sem,
    group_recv_sem,
):
    _, cx, cy, cz = start.shape
    rows = cell.shape[1]
    chord_count = sizes[2]
    me = [lax.axis_index(name) for name in AXES]
    has = [(me[d] > 0, me[d] < sizes[d] - 1) for d in range(3)]
    partner = [(me[d] - 1, me[d] + 1) for d in range(3)]
    peers = [lax.rem(me[2] + i, chord_count) for i in range(chord_count)]

    barrier = pltpu.get_barrier_semaphore()
    greeted = jnp.int32(chord_count - 1)
    for d in range(2):
        for side in range(2):
            greeted = greeted + has[d][side].astype(jnp.int32)

            @pl.when(has[d][side])
            def _(d=d, side=side):
                pl.semaphore_signal(
                    barrier, inc=1, device_id={AXES[d]: partner[d][side]}, device_id_type=MESH
                )

    for i in range(1, chord_count):
        pl.semaphore_signal(barrier, inc=1, device_id={"chord": peers[i]}, device_id_type=MESH)

    load_class = pltpu.make_async_copy(class_hbm, classes, in_sem.at[0])
    load_start = [
        pltpu.make_async_copy(start_hbm.at[c], start.at[c], in_sem.at[1 + c]) for c in range(3)
    ]
    load_source = [
        pltpu.make_async_copy(source_hbm.at[c], source.at[c], in_sem.at[4 + c]) for c in range(3)
    ]
    load_small = [
        pltpu.make_async_copy(cell_hbm, cell, small_sem.at[0]),
        pltpu.make_async_copy(owner_hbm, owner, small_sem.at[1]),
        pltpu.make_async_copy(normal_hbm, normal, small_sem.at[2]),
        pltpu.make_async_copy(mode_hbm, mode, small_sem.at[3]),
    ]
    for copy in [load_class] + load_start + load_source + load_small:
        copy.start()

    for d, halo in ((0, halo_x), (1, halo_y), (2, halo_z)):
        for side in range(2):

            @pl.when(jnp.logical_not(has[d][side]))
            def _(halo=halo, side=side):
                for k in range(SWEEPS):
                    for c in range(3):
                        halo[k, c, side] = jnp.zeros(halo.shape[3:], F32)

    lane = lax.broadcasted_iota(jnp.int32, (cy, cz), 1)
    row = lax.broadcasted_iota(jnp.int32, (cy, cz), 0)
    row8 = lax.broadcasted_iota(jnp.int32, (8, cz), 0)
    lane8 = lax.broadcasted_iota(jnp.int32, (8, cz), 1)
    pair = lane // 2
    edge = (lane == 0) | (lane == cz - 1)
    blocks = cy // 8
    order = [0, cx - 1] + list(range(1, cx - 1))

    def transfer(k, c, d, side):
        other = 1 - side
        if d == 0:
            src, dst = prod.at[k, c, (cx - 1) * side], halo_x.at[k, c, other]
        elif d == 1:
            src, dst = face_y.at[k, c, side], halo_y.at[k, c, other]
        else:
            src, dst = face_z.at[k, c], halo_z.at[k, c, other]
        return pltpu.make_async_remote_copy(
            src_ref=src,
            dst_ref=dst,
            send_sem=send_sem.at[k, c, d, side],
            recv_sem=recv_sem.at[k, c, d, other],
            device_id={AXES[d]: partner[d][side]},
            device_id_type=MESH,
        )

    def send(k, c, d):
        for side in range(2):

            @pl.when(has[d][side])
            def _(side=side):
                transfer(k, c, d, side).start()

    def receive(k, c):
        for d in (2, 1, 0):
            for side in range(2):

                @pl.when(has[d][side])
                def _(d=d, side=side):
                    transfer(k, c, d, 1 - side).wait_recv()

    def emit(k, c, value_at, before_send=None):
        packed = jnp.zeros((cy, cz), F32)
        for place, x in enumerate(order):
            value = value_at(x)
            prod[k, c, x] = value
            face_y[k, c, 0, x : x + 1, :] = value[0:1]
            face_y[k, c, 1, x : x + 1, :] = value[cy - 1 : cy]
            packed = jnp.where(pair == x, pltpu.roll(value, 2 * x + 1, 1), packed)
            if place == 1:
                if before_send is not None:
                    before_send()
                send(k, c, 0)
        tile = packed[0:8]
        stride = cz // blocks
        for b in range(1, blocks):
            tile = tile + pltpu.roll(packed[8 * b : 8 * b + 8], stride * b, 1)
        face_z[k, c] = tile
        send(k, c, 2)
        send(k, c, 1)

    def interior(k, c):
        for x in range(cx):
            here = prod[k, c, x]
            if x == 0:
                span_sum = prod[k, c, 1]
            elif x == cx - 1:
                span_sum = prod[k, c, cx - 2]
            else:
                span_sum = prod[k, c, x - 1] + prod[k, c, x + 1]
            pitch_sum = jnp.where(row == 0, 0.0, pltpu.roll(here, 1, 0)) + jnp.where(
                row == cy - 1, 0.0, pltpu.roll(here, cy - 1, 0)
            )
            chord_sum = jnp.where(lane == 0, 0.0, pltpu.roll(here, 1, 1)) + jnp.where(
                lane == cz - 1, 0.0, pltpu.roll(here, cz - 1, 1)
            )
            sums = (span_sum, pitch_sum, chord_sum)
            total = span_sum + pitch_sum + chord_sum + (OWN_WEIGHT - OFF_WEIGHT) * sums[c]
            prod[k + 1, c, x] = KEEP * here + STEP * (source[c, x] + total)

    def finished(k, c):
        left, right = halo_z[k, c, 0], halo_z[k, c, 1]
        joined = jnp.where(lane8 % 2 == 0, left, pltpu.roll(right, cz - 2, 1))
        joined = (STEP * weight(c, 2)) * joined
        stride = cz // blocks
        spread = jnp.concatenate(
            [joined] + [pltpu.roll(joined, cz - stride * b, 1) for b in range(1, blocks)], axis=0
        )

        def value_at(x):
            value = prod[k + 1, c, x]
            turned = spread if x == 0 else pltpu.roll(spread, cz - 2 * x, 1)
            value = value + jnp.where(edge, turned, 0.0)
            if x == 0:
                value = value + (STEP * weight(c, 0)) * halo_x[k, c, 0]
            if x == cx - 1:
                value = value + (STEP * weight(c, 0)) * halo_x[k, c, 1]
            low = (STEP * weight(c, 1)) * halo_y[k, c, 0, x : x + 1, :]
            high = (STEP * weight(c, 1)) * halo_y[k, c, 1, x : x + 1, :]
            first = value[0:8] + jnp.where(row8 == 0, low, 0.0)
            last = value[cy - 8 : cy] + jnp.where(row8 == 7, high, 0.0)
            return jnp.concatenate([first, value[8 : cy - 8], last], axis=0)

        return value_at

    load_class.wait()

    def first_value(c):
        def value_at(x):
            if c == 0:
                number = classes[x]
                level = jnp.full((cy, cz), table[0], F32)
                for i in range(1, table.shape[0]):
                    level = jnp.where(number == i, table[i], level)
                stiff[x] = level
            else:
                level = stiff[x]
            return level * start[c, x]

        return value_at

    for c in range(3):
        load_start[c].wait()
        meet = (lambda: pl.semaphore_wait(barrier, greeted)) if c == 0 else None
        emit(0, c, first_value(c), meet)
    for c in range(3):
        load_source[c].wait()
        interior(0, c)

    for copy in load_small:
        copy.wait()
    depth_of = cell[...] % cz
    plane_of = cell[...] // cz
    span_of = plane_of // cy
    pitch_of = plane_of % cy

    def build_tables():
        depth = lax.broadcasted_iota(jnp.int32, (cz, rows), 0)
        hot = jnp.where(depth == depth_of, 1.0, 0.0).astype(BF16)
        depth_hot[0:cz, :] = hot
        depth_hot[cz : 2 * cz, :] = hot
        for x in range(cx):
            inverse[x] = 1.0 / stiff[x]

    def build_patches():
        patch = lax.broadcasted_iota(jnp.int32, (PATCH_DEV, rows), 0)
        for j in range(chord_count):
            hot = jnp.where(patch == owner[...] - PATCH_DEV * j, 1.0, 0.0).astype(BF16)
            patch_hot[PATCH_DEV * j : PATCH_DEV * (j + 1), :] = hot

    build_tables()
    for k in range(SWEEPS - 1):
        for c in range(3):
            receive(k, c)
            emit(k + 1, c, finished(k, c))
            interior(k + 1, c)
        if k == 0:
            build_patches()

    width = 256
    parts = [jnp.zeros((1, width), F32) for _ in range(rows // width)]
    store = []
    k = SWEEPS - 1
    for c in range(3):
        receive(k, c)
        value_at = finished(k, c)
        for x in range(cx):
            value = value_at(x)
            result[c, x] = value * inverse[x]
            high, low = split(value)
            pieces[c, cy * x : cy * (x + 1), 0:cz] = high
            pieces[c, cy * x : cy * (x + 1), cz : 2 * cz] = low
        copy = pltpu.make_async_copy(result.at[c], adjoint_hbm.at[c], out_sem.at[c])
        copy.start()
        store.append(copy)
        for n in range(rows // width):
            cut = slice(width * n, width * (n + 1))
            picked = jnp.dot(
                pieces[c], depth_hot[:, cut], preferred_element_type=F32
            )
            chosen = picked[0:cy]
            for x in range(1, cx):
                chosen = jnp.where(
                    span_of[:, cut] == x, picked[cy * x : cy * (x + 1)], chosen
                )
            place = lax.broadcasted_iota(jnp.int32, (cy, width), 0)
            chosen = jnp.where(place == pitch_of[:, cut], chosen, 0.0)
            traction = jnp.sum(chosen, axis=0, keepdims=True)
            parts[n] = parts[n] + normal[c : c + 1, cut] * traction

    contribution = jnp.concatenate(
        [mode[:, width * n : width * (n + 1)] * parts[n] for n in range(rows // width)], axis=1
    )
    high, low = split(contribution)
    both = jnp.concatenate([high, low], axis=0)
    grouped = lax.dot_general(
        both, patch_hot[...], (((1,), (1,)), ((), ())), preferred_element_type=F32
    )
    grouped = grouped[0:MODES] + grouped[MODES : 2 * MODES]
    for j in range(chord_count):
        group_send[j] = grouped[:, PATCH_DEV * j : PATCH_DEV * (j + 1)]

    exchange = []
    for i in range(1, chord_count):
        copy = pltpu.make_async_remote_copy(
            src_ref=group_send.at[peers[i]],
            dst_ref=group_recv.at[i],
            send_sem=group_send_sem.at[i],
            recv_sem=group_recv_sem.at[i],
            device_id={"chord": peers[i]},
            device_id_type=MESH,
        )
        copy.start()
        exchange.append(copy)

    for d in range(3):
        for side in range(2):

            @pl.when(has[d][side])
            def _(d=d, side=side):
                for k in range(SWEEPS):
                    for c in range(3):
                        transfer(k, c, d, side).wait_send()

    total = group_send[me[2]]
    for i, copy in enumerate(exchange):
        copy.wait()
        total = total + group_recv[i + 1]
    patch_out[...] = total
    for copy in store:
        copy.wait()


def body(sizes, start, source, classes, table, cell, owner, normal, mode):
    _, cx, cy, cz = start.shape
    rows = cell.shape[0]
    chord_count = sizes[2]
    hbm = pl.BlockSpec(memory_space=pl.ANY)
    vmem = pltpu.VMEM
    dma = pltpu.SemaphoreType.DMA
    return pl.pallas_call(
        functools.partial(kernel, sizes),
        out_shape=(
            jax.ShapeDtypeStruct(start.shape, F32),
            jax.ShapeDtypeStruct((MODES, PATCH_DEV), F32),
        ),
        in_specs=[hbm, hbm, hbm, pl.BlockSpec(memory_space=pltpu.SMEM), hbm, hbm, hbm, hbm],
        out_specs=(hbm, pl.BlockSpec(memory_space=pltpu.VMEM)),
        scratch_shapes=[
            vmem(start.shape, F32),
            vmem(start.shape, F32),
            vmem((cx, cy, cz), jnp.int32),
            vmem((1, rows), jnp.int32),
            vmem((1, rows), jnp.int32),
            vmem((3, rows), F32),
            vmem((MODES, rows), F32),
            vmem((cx, cy, cz), F32),
            vmem((cx, cy, cz), F32),
            vmem((SWEEPS + 1, 3, cx, cy, cz), F32),
            vmem((SWEEPS, 3, 2, cy, cz), F32),
            vmem((SWEEPS, 3, 2, cx, cz), F32),
            vmem((SWEEPS, 3, 2, 8, cz), F32),
            vmem((SWEEPS, 3, 2, cx, cz), F32),
            vmem((SWEEPS, 3, 8, cz), F32),
            vmem(start.shape, F32),
            vmem((3, cx * cy, 2 * cz), BF16),
            vmem((2 * cz, rows), BF16),
            vmem((chord_count * PATCH_DEV, rows), BF16),
            vmem((chord_count, MODES, PATCH_DEV), F32),
            vmem((chord_count, MODES, PATCH_DEV), F32),
            dma((7,)),
            dma((4,)),
            dma((3,)),
            dma((SWEEPS, 3, 3, 2)),
            dma((SWEEPS, 3, 3, 2)),
            dma((chord_count,)),
            dma((chord_count,)),
        ],
        compiler_params=pltpu.CompilerParams(
            collective_id=0, has_side_effects=True, vmem_limit_bytes=56 * 1024 * 1024
        ),
        cost_estimate=pl.CostEstimate(
            flops=2 * 1024 * 1024 * 1024, bytes_accessed=3 * 1024 * 1024, transcendentals=0
        ),
    )(
        start,
        source,
        classes,
        table,
        cell.reshape(1, rows),
        owner.reshape(1, rows),
        normal,
        mode,
    )


def solution(mesh):
    sizes = tuple(mesh.shape[name] for name in AXES)
    field = P(None, "span", "pitch", "chord")
    listing = P(None, AXES)
    in_specs = (field, field, P(*AXES), P(), P(AXES), P(AXES, None), listing, listing)
    return jax.shard_map(
        functools.partial(body, sizes),
        mesh=mesh,
        in_specs=in_specs,
        out_specs=(field, listing),
        check_vma=False,
    )
```

time: 126 us -> 25.6 us (0.20)
  the two profiles are of different devices: /device:TPU:6 before, /device:TPU:0 now
where the time goes in v1:
time: 25.6 us; the launch traced here: 25.5 us
  Pallas kernels  22.2 us (87%)
  local copies, waits for them, and re-layouts  2.66 us (10%)
  between operations  0.65 us (3%)
    pallas_call x1, Pallas kernels, body(): pl.pallas_call(functools.partial(kernel, sizes), out_shape=(jax.ShapeDtyp...  22.2 us
    unnamed x4, local copies, waits for them, and re-layouts  2.66 us

profile of v1, /device:TPU:0, one launch (start us, length us, event | category | flops | bytes accessed | tf_op | source)
XLA Modules:
  0.0 25.5 jit_solution(10094791186776629902)
XLA Ops:
  0.6 22.2 %shard_map.95 = (f32[3,16,32,128]{3,2,1,0:T(8,128)}, f32[8,128]{1,0:T(8,128)}) custom-call(f32[3,16,32,128]{3,2,1,0:T(8,128)} %start_hbm.1, f32[3,16,32,128]{3,2,1,0:T(8,128)} %source_hbm.1, s32[16,32,128]{2,1,0:T(8,128)} %class_hbm.1, f32[8]{0:T(128)} %table.1, s32[1,1024]{1,0:T(1,128)} %bitcast.2, s32[1,1024]{1,0:T(1,128)} %bitcast.3, ...), custom_call_target="tpu_custom_call" | custom-call | flops 2147483648 | bytes 3145728 | tf_op jit(solution)/shard_map/pallas_call | solution.py:364
  22.8 0.0 copy-start
  22.8 2.1 %copy.12 = f32[3,16,32,128]{3,2,1,0:T(8,128)} copy(f32[3,16,32,128]{3,2,1,0:T(8,128)} %get-tuple-element.4) | data formatting | bytes 1572864
  24.9 0.0 copy-done
  24.9 0.6 %copy.13 = f32[8,128]{1,0:T(8,128)} copy(f32[8,128]{1,0:T(8,128)S(1)} %copy-done) | data formatting | bytes 8192
Async XLA Ops:
  22.8 2.1 %copy-start = (f32[8,128]{1,0:T(8,128)S(1)}, f32[8,128]{1,0:T(8,128)}, u32[]{:S(2)}) copy-start(f32[8,128]{1,0:T(8,128)} %get-tuple-element.5) | copy-start | bytes 12292

commit v2 on v1

--- a/solution.py
+++ b/solution.py
@@ -22,8 +22,8 @@
 BF16 = jnp.bfloat16
 
 
-def weight(component, dim):
-    return OWN_WEIGHT if component == dim else OFF_WEIGHT
+def step_weight(component, dim):
+    return jnp.where(component == dim, F32(STEP * OWN_WEIGHT), F32(STEP * OFF_WEIGHT))
 
 
 def split(value):
@@ -42,7 +42,7 @@
     owner_hbm,
     normal_hbm,
     mode_hbm,
-    adjoint_hbm,
+    adjoint_out,
     patch_out,
     start,
     source,
@@ -59,7 +59,7 @@
     halo_z,
     face_y,
     face_z,
-    result,
+    traction,
     pieces,
     depth_hot,
     patch_hot,
@@ -67,7 +67,6 @@
     group_recv,
     in_sem,
     small_sem,
-    out_sem,
     send_sem,
     recv_sem,
     group_send_sem,
@@ -162,7 +161,7 @@
                 def _(d=d, side=side):
                     transfer(k, c, d, 1 - side).wait_recv()
 
-    def emit(k, c, value_at, before_send=None):
+    def emit(k, c, value_at):
         packed = jnp.zeros((cy, cz), F32)
         for place, x in enumerate(order):
             value = value_at(x)
@@ -171,8 +170,6 @@
             face_y[k, c, 1, x : x + 1, :] = value[cy - 1 : cy]
             packed = jnp.where(pair == x, pltpu.roll(value, 2 * x + 1, 1), packed)
             if place == 1:
-                if before_send is not None:
-                    before_send()
                 send(k, c, 0)
         tile = packed[0:8]
         stride = cz // blocks
@@ -183,6 +180,7 @@
         send(k, c, 1)
 
     def interior(k, c):
+        weights = [step_weight(c, d) for d in range(3)]
         for x in range(cx):
             here = prod[k, c, x]
             if x == 0:
@@ -197,14 +195,14 @@
             chord_sum = jnp.where(lane == 0, 0.0, pltpu.roll(here, 1, 1)) + jnp.where(
                 lane == cz - 1, 0.0, pltpu.roll(here, cz - 1, 1)
             )
-            sums = (span_sum, pitch_sum, chord_sum)
-            total = span_sum + pitch_sum + chord_sum + (OWN_WEIGHT - OFF_WEIGHT) * sums[c]
-            prod[k + 1, c, x] = KEEP * here + STEP * (source[c, x] + total)
+            around = weights[0] * span_sum + weights[1] * pitch_sum + weights[2] * chord_sum
+            prod[k + 1, c, x] = KEEP * here + STEP * source[c, x] + around
 
     def finished(k, c):
         left, right = halo_z[k, c, 0], halo_z[k, c, 1]
         joined = jnp.where(lane8 % 2 == 0, left, pltpu.roll(right, cz - 2, 1))
-        joined = (STEP * weight(c, 2)) * joined
+        weights = [step_weight(c, d) for d in range(3)]
+        joined = weights[2] * joined
         stride = cz // blocks
         spread = jnp.concatenate(
             [joined] + [pltpu.roll(joined, cz - stride * b, 1) for b in range(1, blocks)], axis=0
@@ -215,11 +213,11 @@
             turned = spread if x == 0 else pltpu.roll(spread, cz - 2 * x, 1)
             value = value + jnp.where(edge, turned, 0.0)
             if x == 0:
-                value = value + (STEP * weight(c, 0)) * halo_x[k, c, 0]
+                value = value + weights[0] * halo_x[k, c, 0]
             if x == cx - 1:
-                value = value + (STEP * weight(c, 0)) * halo_x[k, c, 1]
-            low = (STEP * weight(c, 1)) * halo_y[k, c, 0, x : x + 1, :]
-            high = (STEP * weight(c, 1)) * halo_y[k, c, 1, x : x + 1, :]
+                value = value + weights[0] * halo_x[k, c, 1]
+            low = weights[1] * halo_y[k, c, 0, x : x + 1, :]
+            high = weights[1] * halo_y[k, c, 1, x : x + 1, :]
             first = value[0:8] + jnp.where(row8 == 0, low, 0.0)
             last = value[cy - 8 : cy] + jnp.where(row8 == 7, high, 0.0)
             return jnp.concatenate([first, value[8 : cy - 8], last], axis=0)
@@ -228,27 +226,26 @@
 
     load_class.wait()
 
-    def first_value(c):
-        def value_at(x):
-            if c == 0:
-                number = classes[x]
-                level = jnp.full((cy, cz), table[0], F32)
-                for i in range(1, table.shape[0]):
-                    level = jnp.where(number == i, table[i], level)
-                stiff[x] = level
-            else:
-                level = stiff[x]
-            return level * start[c, x]
-
-        return value_at
-
-    for c in range(3):
-        load_start[c].wait()
-        meet = (lambda: pl.semaphore_wait(barrier, greeted)) if c == 0 else None
-        emit(0, c, first_value(c), meet)
-    for c in range(3):
-        load_source[c].wait()
+    for x in range(cx):
+        number = classes[x]
+        level = jnp.full((cy, cz), table[0], F32)
+        for i in range(1, table.shape[0]):
+            level = jnp.where(number == i, table[i], level)
+        stiff[x] = level
+    pl.semaphore_wait(barrier, greeted)
+
+    def first(c, _):
+        pltpu.make_async_copy(start_hbm.at[c], start.at[c], in_sem.at[1 + c]).wait()
+        emit(0, c, lambda x: stiff[x] * start[c, x])
+        return 0
+
+    def inner(c, _):
+        pltpu.make_async_copy(source_hbm.at[c], source.at[c], in_sem.at[4 + c]).wait()
         interior(0, c)
+        return 0
+
+    lax.fori_loop(0, 3, first, 0)
+    lax.fori_loop(0, 3, inner, 0)
 
     for copy in load_small:
         copy.wait()
@@ -272,35 +269,31 @@
             patch_hot[PATCH_DEV * j : PATCH_DEV * (j + 1), :] = hot
 
     build_tables()
-    for k in range(SWEEPS - 1):
-        for c in range(3):
-            receive(k, c)
-            emit(k + 1, c, finished(k, c))
-            interior(k + 1, c)
-        if k == 0:
-            build_patches()
+    build_patches()
+
+    def sweep(number, _):
+        k, c = number // 3, number % 3
+        receive(k, c)
+        emit(k + 1, c, finished(k, c))
+        interior(k + 1, c)
+        return 0
+
+    lax.fori_loop(0, 3 * (SWEEPS - 1), sweep, 0)
 
     width = 256
-    parts = [jnp.zeros((1, width), F32) for _ in range(rows // width)]
-    store = []
-    k = SWEEPS - 1
-    for c in range(3):
-        receive(k, c)
-        value_at = finished(k, c)
+
+    def last(c, _):
+        receive(SWEEPS - 1, c)
+        value_at = finished(SWEEPS - 1, c)
         for x in range(cx):
             value = value_at(x)
-            result[c, x] = value * inverse[x]
+            adjoint_out[c, x] = value * inverse[x]
             high, low = split(value)
             pieces[c, cy * x : cy * (x + 1), 0:cz] = high
             pieces[c, cy * x : cy * (x + 1), cz : 2 * cz] = low
-        copy = pltpu.make_async_copy(result.at[c], adjoint_hbm.at[c], out_sem.at[c])
-        copy.start()
-        store.append(copy)
         for n in range(rows // width):
             cut = slice(width * n, width * (n + 1))
-            picked = jnp.dot(
-                pieces[c], depth_hot[:, cut], preferred_element_type=F32
-            )
+            picked = jnp.dot(pieces[c], depth_hot[:, cut], preferred_element_type=F32)
             chosen = picked[0:cy]
             for x in range(1, cx):
                 chosen = jnp.where(
@@ -308,12 +301,13 @@
                 )
             place = lax.broadcasted_iota(jnp.int32, (cy, width), 0)
             chosen = jnp.where(place == pitch_of[:, cut], chosen, 0.0)
-            traction = jnp.sum(chosen, axis=0, keepdims=True)
-            parts[n] = parts[n] + normal[c : c + 1, cut] * traction
-
-    contribution = jnp.concatenate(
-        [mode[:, width * n : width * (n + 1)] * parts[n] for n in range(rows // width)], axis=1
-    )
+            traction[c, :, cut] = jnp.sum(chosen, axis=0, keepdims=True)
+        return 0
+
+    lax.fori_loop(0, 3, last, 0)
+    normal_part = sum(normal[c : c + 1, :] * traction[c] for c in range(3))
+
+    contribution = mode[...] * normal_part
     high, low = split(contribution)
     both = jnp.concatenate([high, low], axis=0)
     grouped = lax.dot_general(
@@ -350,7 +344,16 @@
         copy.wait()
         total = total + group_recv[i + 1]
     patch_out[...] = total
-    for copy in store:
+
+
+def write(adjoint, patches, adjoint_hbm, patch_hbm, sem):
+    copies = [
+        pltpu.make_async_copy(adjoint, adjoint_hbm, sem.at[0]),
+        pltpu.make_async_copy(patches, patch_hbm, sem.at[1]),
+    ]
+    for copy in copies:
+        copy.start()
+    for copy in copies:
         copy.wait()
 
 
@@ -359,16 +362,14 @@
     rows = cell.shape[0]
     chord_count = sizes[2]
     hbm = pl.BlockSpec(memory_space=pl.ANY)
+    main = pl.BlockSpec(memory_space=pltpu.HBM)
     vmem = pltpu.VMEM
     dma = pltpu.SemaphoreType.DMA
-    return pl.pallas_call(
+    adjoint, patches = pl.pallas_call(
         functools.partial(kernel, sizes),
-        out_shape=(
-            jax.ShapeDtypeStruct(start.shape, F32),
-            jax.ShapeDtypeStruct((MODES, PATCH_DEV), F32),
-        ),
-        in_specs=[hbm, hbm, hbm, pl.BlockSpec(memory_space=pltpu.SMEM), hbm, hbm, hbm, hbm],
-        out_specs=(hbm, pl.BlockSpec(memory_space=pltpu.VMEM)),
+        out_shape=(vmem(start.shape, F32), vmem((MODES, PATCH_DEV), F32)),
+        in_specs=[main, main, main, pl.BlockSpec(memory_space=pltpu.SMEM), main, main, main, main],
+        out_specs=(pl.BlockSpec(memory_space=vmem), pl.BlockSpec(memory_space=vmem)),
         scratch_shapes=[
             vmem(start.shape, F32),
             vmem(start.shape, F32),
@@ -385,7 +386,7 @@
             vmem((SWEEPS, 3, 2, 8, cz), F32),
             vmem((SWEEPS, 3, 2, cx, cz), F32),
             vmem((SWEEPS, 3, 8, cz), F32),
-            vmem(start.shape, F32),
+            vmem((3, 1, rows), F32),
             vmem((3, cx * cy, 2 * cz), BF16),
             vmem((2 * cz, rows), BF16),
             vmem((chord_count * PATCH_DEV, rows), BF16),
@@ -393,14 +394,13 @@
             vmem((chord_count, MODES, PATCH_DEV), F32),
             dma((7,)),
             dma((4,)),
-            dma((3,)),
             dma((SWEEPS, 3, 3, 2)),
             dma((SWEEPS, 3, 3, 2)),
             dma((chord_count,)),
             dma((chord_count,)),
         ],
         compiler_params=pltpu.CompilerParams(
-            collective_id=0, has_side_effects=True, vmem_limit_bytes=56 * 1024 * 1024
+            collective_id=0, has_side_effects=True, vmem_limit_bytes=63 * 1024 * 1024
         ),
         cost_estimate=pl.CostEstimate(
             flops=2 * 1024 * 1024 * 1024, bytes_accessed=3 * 1024 * 1024, transcendentals=0
@@ -415,6 +415,16 @@
         normal,
         mode,
     )
+    return pl.pallas_call(
+        write,
+        out_shape=(
+            jax.ShapeDtypeStruct(adjoint.shape, F32),
+            jax.ShapeDtypeStruct(patches.shape, F32),
+        ),
+        in_specs=[hbm, hbm],
+        out_specs=(hbm, hbm),
+        scratch_shapes=[dma((2,))],
+    )(adjoint, patches)
 
 
 def solution(mesh):

time: 25.6 us -> 49.1 us (1.92)
  Pallas kernels: 22.2 us -> 46.8 us
  local copies, waits for them, and re-layouts: 2.66 us -> 1.47 us
    pallas_call x1 -> x2, Pallas kernels: 22.2 us -> 46.8 us  [the longest x1 25.1 us: body(): pl.pallas_call(write, out_shape=(jax.ShapeDtypeStruct(adjoint.shape, F32)...]
    unnamed x4, local copies, waits for them, and re-layouts: 2.66 us -> 1.47 us
where the time goes in v2:
time: 49.1 us; the launch traced here: 48.9 us
  Pallas kernels  46.8 us (95%)
  local copies, waits for them, and re-layouts  1.47 us (3%)
  between operations  0.65 us (1%)
    pallas_call x1, Pallas kernels, body(): pl.pallas_call(write, out_shape=(jax.ShapeDtypeStruct(adjoint.shape, F32)...  25.1 us
    pallas_call x1, Pallas kernels, body(): pl.pallas_call(functools.partial(kernel, sizes), out_shape=(vmem(start.sh...  21.8 us
    unnamed x4, local copies, waits for them, and re-layouts  1.47 us

profile of v2, /device:TPU:0, one launch (start us, length us, event | category | flops | bytes accessed | tf_op | source)
XLA Modules:
  0.0 48.9 jit_solution(3846326490953193455)
XLA Ops:
  0.6 21.8 %shard_map.95 = (f32[3,16,32,128]{3,2,1,0:T(8,128)S(1)}, f32[8,128]{1,0:T(8,128)S(1)}) custom-call(f32[3,16,32,128]{3,2,1,0:T(8,128)} %start_hbm.1, f32[3,16,32,128]{3,2,1,0:T(8,128)} %source_hbm.1, s32[16,32,128]{2,1,0:T(8,128)} %class_hbm.1, f32[8]{0:T(128)} %table.1, s32[1,1024]{1,0:T(1,128)} %bitcast.2, s32[1,1024]{1,0:T(1,128)} %bitcast.3, ...), custom_call_target="tpu_custom_call" | custom-call | flops 2147483648 | bytes 3145728 | tf_op jit(solution)/shard_map/pallas_call | solution.py:368
  22.4 0.0 copy-start
  22.4 0.9 %copy-done = f32[3,16,32,128]{3,2,1,0:T(8,128)} copy-done((f32[3,16,32,128]{3,2,1,0:T(8,128)}, f32[3,16,32,128]{3,2,1,0:T(8,128)S(1)}, u32[]{:S(2)}) %copy-start) | copy-done | bytes 786456
  23.3 0.0 copy-start.1
  23.3 0.6 %copy-done.1 = f32[8,128]{1,0:T(8,128)} copy-done((f32[8,128]{1,0:T(8,128)}, f32[8,128]{1,0:T(8,128)S(1)}, u32[]{:S(2)}) %copy-start.1) | copy-done | bytes 4120
  23.9 25.1 %shard_map.96 = (f32[3,16,32,128]{3,2,1,0:T(8,128)}, f32[8,128]{1,0:T(8,128)}) custom-call(f32[3,16,32,128]{3,2,1,0:T(8,128)} %copy-done, f32[8,128]{1,0:T(8,128)} %copy-done.1), custom_call_target="tpu_custom_call" | custom-call | tf_op jit(solution)/shard_map/pallas_call | solution.py:418
Async XLA Ops:
  22.4 0.9 %copy-start = (f32[3,16,32,128]{3,2,1,0:T(8,128)}, f32[3,16,32,128]{3,2,1,0:T(8,128)S(1)}, u32[]{:S(2)}) copy-start(f32[3,16,32,128]{3,2,1,0:T(8,128)S(1)} %get-tuple-element.4.adjoint) | copy-start | bytes 2359300
  23.3 0.6 %copy-start.1 = (f32[8,128]{1,0:T(8,128)}, f32[8,128]{1,0:T(8,128)S(1)}, u32[]{:S(2)}) copy-start(f32[8,128]{1,0:T(8,128)S(1)} %get-tuple-element.5.patches) | copy-start | bytes 12292

commit v3 on v2

--- a/solution.py
+++ b/solution.py
@@ -346,26 +346,14 @@
     patch_out[...] = total
 
 
-def write(adjoint, patches, adjoint_hbm, patch_hbm, sem):
-    copies = [
-        pltpu.make_async_copy(adjoint, adjoint_hbm, sem.at[0]),
-        pltpu.make_async_copy(patches, patch_hbm, sem.at[1]),
-    ]
-    for copy in copies:
-        copy.start()
-    for copy in copies:
-        copy.wait()
-
-
 def body(sizes, start, source, classes, table, cell, owner, normal, mode):
     _, cx, cy, cz = start.shape
     rows = cell.shape[0]
     chord_count = sizes[2]
-    hbm = pl.BlockSpec(memory_space=pl.ANY)
     main = pl.BlockSpec(memory_space=pltpu.HBM)
     vmem = pltpu.VMEM
     dma = pltpu.SemaphoreType.DMA
-    adjoint, patches = pl.pallas_call(
+    return pl.pallas_call(
         functools.partial(kernel, sizes),
         out_shape=(vmem(start.shape, F32), vmem((MODES, PATCH_DEV), F32)),
         in_specs=[main, main, main, pl.BlockSpec(memory_space=pltpu.SMEM), main, main, main, main],
@@ -415,17 +403,6 @@
         normal,
         mode,
     )
-    return pl.pallas_call(
-        write,
-        out_shape=(
-            jax.ShapeDtypeStruct(adjoint.shape, F32),
-            jax.ShapeDtypeStruct(patches.shape, F32),
-        ),
-        in_specs=[hbm, hbm],
-        out_specs=(hbm, hbm),
-        scratch_shapes=[dma((2,))],
-    )(adjoint, patches)
-
 
 def solution(mesh):
     sizes = tuple(mesh.shape[name] for name in AXES)

time: 49.1 us -> 24 us (0.49)
  Pallas kernels: 46.8 us -> 21.8 us
    pallas_call x1 -> x0, Pallas kernels: 25.1 us -> none  [body(): pl.pallas_call(write, out_shape=(jax.ShapeDtypeStruct(adjoint.shape, F32)...]
    unnamed x4 -> x2, local copies, waits for them, and re-layouts: 1.47 us -> 1.47 us
where the time goes in v3:
time: 24 us; the launch traced here: 23.9 us
  Pallas kernels  21.8 us (91%)
  local copies, waits for them, and re-layouts  1.47 us (6%)
  between operations  0.64 us (3%)
    pallas_call x1, Pallas kernels, body(): pl.pallas_call(functools.partial(kernel, sizes), out_shape=(vmem(start.sh...  21.8 us
    unnamed x2, local copies, waits for them, and re-layouts  1.47 us

profile of v3, /device:TPU:0, one launch (start us, length us, event | category | flops | bytes accessed | tf_op | source)
XLA Modules:
  0.0 23.9 jit_solution(5228244253325549345)
XLA Ops:
  0.6 21.8 %shard_map.95 = (f32[3,16,32,128]{3,2,1,0:T(8,128)S(1)}, f32[8,128]{1,0:T(8,128)S(1)}) custom-call(f32[3,16,32,128]{3,2,1,0:T(8,128)} %start_hbm.1, f32[3,16,32,128]{3,2,1,0:T(8,128)} %source_hbm.1, s32[16,32,128]{2,1,0:T(8,128)} %class_hbm.1, f32[8]{0:T(128)} %table.1, s32[1,1024]{1,0:T(1,128)} %bitcast.2, s32[1,1024]{1,0:T(1,128)} %bitcast.3, ...), custom_call_target="tpu_custom_call" | custom-call | flops 2147483648 | bytes 3145728 | tf_op jit(solution)/shard_map/pallas_call | solution.py:356
  22.4 0.9 %copy.12 = f32[3,16,32,128]{3,2,1,0:T(8,128)} copy(f32[3,16,32,128]{3,2,1,0:T(8,128)S(1)} %get-tuple-element.2) | data formatting | bytes 1572864
  23.3 0.6 %copy.13 = f32[8,128]{1,0:T(8,128)} copy(f32[8,128]{1,0:T(8,128)S(1)} %get-tuple-element.3) | data formatting | bytes 8192

commit v4 on v3

--- a/solution.py
+++ b/solution.py
@@ -118,7 +118,7 @@
             def _(halo=halo, side=side):
                 for k in range(SWEEPS):
                     for c in range(3):
-                        halo[k, c, side] = jnp.zeros(halo.shape[3:], F32)
+                        halo[k, side, c] = jnp.zeros(halo.shape[3:], F32)
 
     lane = lax.broadcasted_iota(jnp.int32, (cy, cz), 1)
     row = lax.broadcasted_iota(jnp.int32, (cy, cz), 0)
@@ -129,55 +129,72 @@
     blocks = cy // 8
     order = [0, cx - 1] + list(range(1, cx - 1))
 
-    def transfer(k, c, d, side):
+    def remote(src, dst, k, slot, d, side):
         other = 1 - side
-        if d == 0:
-            src, dst = prod.at[k, c, (cx - 1) * side], halo_x.at[k, c, other]
-        elif d == 1:
-            src, dst = face_y.at[k, c, side], halo_y.at[k, c, other]
-        else:
-            src, dst = face_z.at[k, c], halo_z.at[k, c, other]
         return pltpu.make_async_remote_copy(
             src_ref=src,
             dst_ref=dst,
-            send_sem=send_sem.at[k, c, d, side],
-            recv_sem=recv_sem.at[k, c, d, other],
-            device_id={AXES[d]: partner[d][side]},
+            send_sem=send_sem.at[k, slot, side],
+            recv_sem=recv_sem.at[k, slot, other],
+            device_id={AXES[d]: me[d] - 1 + 2 * side},
             device_id_type=MESH,
         )
 
-    def send(k, c, d):
+    def span_transfer(k, c, side):
+        src = prod.at[k, c, (cx - 1) * side]
+        return remote(src, halo_x.at[k, 1 - side, c], k, c, 0, side)
+
+    def pitch_transfer(k, side):
+        return remote(face_y.at[k, side], halo_y.at[k, 1 - side], k, 3, 1, side)
+
+    def chord_transfer(k, side):
+        return remote(face_z.at[k], halo_z.at[k, 1 - side], k, 4, 2, side)
+
+    def on_span(act):
+        if sizes[0] == 2:
+            act(1 - me[0])
+            return
         for side in range(2):
 
-            @pl.when(has[d][side])
+            @pl.when(has[0][side])
             def _(side=side):
-                transfer(k, c, d, side).start()
-
-    def receive(k, c):
-        for d in (2, 1, 0):
+                act(side)
+
+    def on_rest(act):
+        for d, move in ((2, chord_transfer), (1, pitch_transfer)):
             for side in range(2):
 
                 @pl.when(has[d][side])
-                def _(d=d, side=side):
-                    transfer(k, c, d, 1 - side).wait_recv()
+                def _(move=move, side=side):
+                    act(move, side)
+
+    def send_span(k, c):
+        on_span(lambda side: span_transfer(k, c, side).start())
+
+    def send_rest(k):
+        on_rest(lambda move, side: move(k, side).start())
+
+    def receive_span(k, c):
+        on_span(lambda side: span_transfer(k, c, 1 - side).wait_recv())
+
+    def receive_rest(k):
+        on_rest(lambda move, side: move(k, 1 - side).wait_recv())
 
     def emit(k, c, value_at):
         packed = jnp.zeros((cy, cz), F32)
         for place, x in enumerate(order):
             value = value_at(x)
             prod[k, c, x] = value
-            face_y[k, c, 0, x : x + 1, :] = value[0:1]
-            face_y[k, c, 1, x : x + 1, :] = value[cy - 1 : cy]
+            face_y[k, 0, c, x : x + 1, :] = value[0:1]
+            face_y[k, 1, c, x : x + 1, :] = value[cy - 1 : cy]
             packed = jnp.where(pair == x, pltpu.roll(value, 2 * x + 1, 1), packed)
             if place == 1:
-                send(k, c, 0)
+                send_span(k, c)
         tile = packed[0:8]
         stride = cz // blocks
         for b in range(1, blocks):
             tile = tile + pltpu.roll(packed[8 * b : 8 * b + 8], stride * b, 1)
         face_z[k, c] = tile
-        send(k, c, 2)
-        send(k, c, 1)
 
     def interior(k, c):
         weights = [step_weight(c, d) for d in range(3)]
@@ -199,7 +216,7 @@
             prod[k + 1, c, x] = KEEP * here + STEP * source[c, x] + around
 
     def finished(k, c):
-        left, right = halo_z[k, c, 0], halo_z[k, c, 1]
+        left, right = halo_z[k, 0, c], halo_z[k, 1, c]
         joined = jnp.where(lane8 % 2 == 0, left, pltpu.roll(right, cz - 2, 1))
         weights = [step_weight(c, d) for d in range(3)]
         joined = weights[2] * joined
@@ -213,11 +230,11 @@
             turned = spread if x == 0 else pltpu.roll(spread, cz - 2 * x, 1)
             value = value + jnp.where(edge, turned, 0.0)
             if x == 0:
-                value = value + weights[0] * halo_x[k, c, 0]
+                value = value + weights[0] * halo_x[k, 0, c]
             if x == cx - 1:
-                value = value + weights[0] * halo_x[k, c, 1]
-            low = weights[1] * halo_y[k, c, 0, x : x + 1, :]
-            high = weights[1] * halo_y[k, c, 1, x : x + 1, :]
+                value = value + weights[0] * halo_x[k, 1, c]
+            low = weights[1] * halo_y[k, 0, c, x : x + 1, :]
+            high = weights[1] * halo_y[k, 1, c, x : x + 1, :]
             first = value[0:8] + jnp.where(row8 == 0, low, 0.0)
             last = value[cy - 8 : cy] + jnp.where(row8 == 7, high, 0.0)
             return jnp.concatenate([first, value[8 : cy - 8], last], axis=0)
@@ -245,6 +262,7 @@
         return 0
 
     lax.fori_loop(0, 3, first, 0)
+    send_rest(0)
     lax.fori_loop(0, 3, inner, 0)
 
     for copy in load_small:
@@ -271,19 +289,30 @@
     build_tables()
     build_patches()
 
-    def sweep(number, _):
-        k, c = number // 3, number % 3
-        receive(k, c)
-        emit(k + 1, c, finished(k, c))
-        interior(k + 1, c)
+    def sweep(k, _):
+        receive_rest(k)
+
+        def finish(c, _):
+            receive_span(k, c)
+            emit(k + 1, c, finished(k, c))
+            return 0
+
+        def advance(c, _):
+            interior(k + 1, c)
+            return 0
+
+        lax.fori_loop(0, 3, finish, 0)
+        send_rest(k + 1)
+        lax.fori_loop(0, 3, advance, 0)
         return 0
 
-    lax.fori_loop(0, 3 * (SWEEPS - 1), sweep, 0)
+    lax.fori_loop(0, SWEEPS - 1, sweep, 0)
+    receive_rest(SWEEPS - 1)
 
     width = 256
 
     def last(c, _):
-        receive(SWEEPS - 1, c)
+        receive_span(SWEEPS - 1, c)
         value_at = finished(SWEEPS - 1, c)
         for x in range(cx):
             value = value_at(x)
@@ -330,14 +359,17 @@
         copy.start()
         exchange.append(copy)
 
-    for d in range(3):
-        for side in range(2):
-
-            @pl.when(has[d][side])
-            def _(d=d, side=side):
-                for k in range(SWEEPS):
-                    for c in range(3):
-                        transfer(k, c, d, side).wait_send()
+    def drain_span(side):
+        for k in range(SWEEPS):
+            for c in range(3):
+                span_transfer(k, c, side).wait_send()
+
+    def drain_rest(move, side):
+        for k in range(SWEEPS):
+            move(k, side).wait_send()
+
+    on_span(drain_span)
+    on_rest(drain_rest)
 
     total = group_send[me[2]]
     for i, copy in enumerate(exchange):
@@ -369,10 +401,10 @@
             vmem((cx, cy, cz), F32),
             vmem((cx, cy, cz), F32),
             vmem((SWEEPS + 1, 3, cx, cy, cz), F32),
-            vmem((SWEEPS, 3, 2, cy, cz), F32),
-            vmem((SWEEPS, 3, 2, cx, cz), F32),
-            vmem((SWEEPS, 3, 2, 8, cz), F32),
-            vmem((SWEEPS, 3, 2, cx, cz), F32),
+            vmem((SWEEPS, 2, 3, cy, cz), F32),
+            vmem((SWEEPS, 2, 3, cx, cz), F32),
+            vmem((SWEEPS, 2, 3, 8, cz), F32),
+            vmem((SWEEPS, 2, 3, cx, cz), F32),
             vmem((SWEEPS, 3, 8, cz), F32),
             vmem((3, 1, rows), F32),
             vmem((3, cx * cy, 2 * cz), BF16),
@@ -382,8 +414,8 @@
             vmem((chord_count, MODES, PATCH_DEV), F32),
             dma((7,)),
             dma((4,)),
-            dma((SWEEPS, 3, 3, 2)),
-            dma((SWEEPS, 3, 3, 2)),
+            dma((SWEEPS, 5, 2)),
+            dma((SWEEPS, 5, 2)),
             dma((chord_count,)),
             dma((chord_count,)),
         ],

time: 24 us -> 25.7 us (1.071)
  Pallas kernels: 21.8 us -> 23.5 us
    pallas_call x1, Pallas kernels: 21.8 us -> 23.5 us  [body(): pl.pallas_call(functools.partial(kernel, sizes), out_shape=(vmem(start.sh...]
where the time goes in v4:
time: 25.7 us; the launch traced here: 25.6 us
  Pallas kernels  23.5 us (91%)
  local copies, waits for them, and re-layouts  1.47 us (6%)
  between operations  0.64 us (2%)
    pallas_call x1, Pallas kernels, body(): pl.pallas_call(functools.partial(kernel, sizes), out_shape=(vmem(start.sh...  23.5 us
    unnamed x2, local copies, waits for them, and re-layouts  1.47 us

profile of v4, /device:TPU:0, one launch (start us, length us, event | category | flops | bytes accessed | tf_op | source)
XLA Modules:
  0.0 25.6 jit_solution(1052462296445334559)
XLA Ops:
  0.6 23.5 %shard_map.95 = (f32[3,16,32,128]{3,2,1,0:T(8,128)S(1)}, f32[8,128]{1,0:T(8,128)S(1)}) custom-call(f32[3,16,32,128]{3,2,1,0:T(8,128)} %start_hbm.1, f32[3,16,32,128]{3,2,1,0:T(8,128)} %source_hbm.1, s32[16,32,128]{2,1,0:T(8,128)} %class_hbm.1, f32[8]{0:T(128)} %table.1, s32[1,1024]{1,0:T(1,128)} %bitcast.2, s32[1,1024]{1,0:T(1,128)} %bitcast.3, ...), custom_call_target="tpu_custom_call" | custom-call | flops 2147483648 | bytes 3145728 | tf_op jit(solution)/shard_map/pallas_call | solution.py:388
  24.1 0.9 %copy.12 = f32[3,16,32,128]{3,2,1,0:T(8,128)} copy(f32[3,16,32,128]{3,2,1,0:T(8,128)S(1)} %get-tuple-element.2) | data formatting | bytes 1572864
  25.0 0.6 %copy.13 = f32[8,128]{1,0:T(8,128)} copy(f32[8,128]{1,0:T(8,128)S(1)} %get-tuple-element.3) | data formatting | bytes 8192
